TPU v7x, 256 devices: a whole 4x4x8 slice. The times are simulated.
256 devices in a mesh: dp: 2 (over core), dom: 128 (over y, z, x).
Axes of the slice: x: 4, y: 4, z: 8, core: 2. Of those that a mesh axis runs over, the one named last changes fastest.
Arguments:
- features: bfloat16 [2, 49152, 512], P('dp', 'dom'), may hold values from -12 to 12
- tile_mask: int32 [2, 384, 18], P('dp', 'dom'), may hold values from 0 to 1, as said below
- cotangent: bfloat16 [2, 49152, 512], P('dp', 'dom'), may hold values from -6 to 6
- w_query: bfloat16 [512, 512], replicated, may hold values from -1 to 1
- w_key: bfloat16 [512, 512], replicated, may hold values from -1 to 1
- w_value: bfloat16 [512, 512], replicated, may hold values from -0.25 to 0.25
- w_out: bfloat16 [512, 512], replicated, may hold values from -0.25 to 0.25
Outputs:
- attended: bfloat16 [2, 49152, 512], P('dp', 'dom')
- grad_features: bfloat16 [2, 49152, 512], P('dp', 'dom')
- grad_query: float32 [512, 512], replicated
- grad_key: float32 [512, 512], replicated
- grad_value: float32 [512, 512], replicated
- grad_out: float32 [512, 512], replicated
Inputs may be any that keep to these rules, and one draw needn't show every extreme that they name: `tile_mask`: 0 or 1; the share of ones differs between tile groups, from about a quarter to all.
All inputs are finite; a program needn't handle non-finite values.
Results may differ from a plain program's by a relative error of at most 0.023.
Values may be sent and summed in bfloat16 or wider, within the bound.
A program may use at most 128 MiB of HBM per device.

v0:
```python
import jax
import jax.numpy as jnp
from jax import lax
from jax.sharding import PartitionSpec as P

HEADS = 8
HEAD_DIM = 64
TILE = 128
TILE_DEV = 3
NB = 3
CANDT = 18


def with_halo(block, sides, width):
    for axis, dim in sides:
        count = lax.axis_size(axis)
        forward = [(i, i + 1) for i in range(count - 1)]
        forward.append((count - 1, 0))
        backward = [(target, source) for source, target in forward]
        low = lax.ppermute(
            lax.slice_in_dim(block, block.shape[dim] - width, None, axis=dim), axis, forward
        )
        high = lax.ppermute(lax.slice_in_dim(block, 0, width, axis=dim), axis, backward)
        block = jnp.concatenate([low, block, high], axis=dim)
    return block


def from_partner(value, axis, distance):
    mask = 2**distance
    pairs = [(source, source ^ mask) for source in range(lax.axis_size(axis))]
    return lax.ppermute(value, axis, pairs)


def candidate_blocks(block):
    block_rows = block.shape[0]
    near = with_halo(block, (("dom", 0),), block_rows)
    pieces = [block, near[:block_rows], near[2 * block_rows :]]
    levels = lax.axis_size("dom").bit_length() - 1
    for bit_step in range(NB):
        pieces.append(from_partner(block, "dom", levels - 1 - bit_step))
    return pieces


def returned_sum(grad_parts):
    block_rows = grad_parts.shape[1]
    outgoing = jnp.concatenate([grad_parts[1], grad_parts[2]], 0)
    returned = with_halo(outgoing, (("dom", 0),), block_rows)
    summed = grad_parts[0] + returned[:block_rows] + returned[3 * block_rows :]
    levels = lax.axis_size("dom").bit_length() - 1
    for bit_step in range(NB):
        summed = summed + from_partner(grad_parts[3 + bit_step], "dom", levels - 1 - bit_step)
    return summed


def joined(stacked_parts, width_all):
    return jnp.transpose(stacked_parts, (1, 0, 2)).reshape(stacked_parts.shape[1], width_all)


def per_device(features, tile_mask, cotangent, w_query, w_key, w_value, w_out):
    node_rows = features[0]
    block_rows = node_rows.shape[0]
    width_all = node_rows.shape[1]
    highest = lax.Precision.HIGHEST
    factor = HEAD_DIM ** (-0.5)
    w_both = jnp.concatenate([w_key, w_value], 1)
    q_rows = jnp.dot(node_rows, w_query, preferred_element_type=jnp.float32).astype(jnp.bfloat16)
    kv_rows = jnp.dot(node_rows, w_both, preferred_element_type=jnp.float32).astype(jnp.bfloat16)
    cand_kv = jnp.concatenate(candidate_blocks(kv_rows), 0)
    key_count = cand_kv.shape[0]
    keys_all = cand_kv[:, :width_all]
    values_all = cand_kv[:, width_all:]
    own_tile = jnp.arange(CANDT)[None, :] == jnp.arange(TILE_DEV)[:, None]
    live_tiles = (tile_mask[0] == 1) | own_tile
    masking = jnp.where(live_tiles, 0.0, -1e30).astype(jnp.float32)
    cot_rows = cotangent[0]
    grad_o = jnp.dot(cot_rows, w_out.T, preferred_element_type=jnp.float32).astype(jnp.bfloat16)
    pair_cols = 2 * HEAD_DIM

    def head_pair(pair_index):
        col_start = pair_index * pair_cols
        q_pair = lax.dynamic_slice_in_dim(q_rows, col_start, pair_cols, 1).reshape(
            block_rows, 2, HEAD_DIM
        )
        k_pair = lax.dynamic_slice_in_dim(keys_all, col_start, pair_cols, 1).reshape(
            key_count, 2, HEAD_DIM
        )
        v_pair = lax.dynamic_slice_in_dim(values_all, col_start, pair_cols, 1).reshape(
            key_count, 2, HEAD_DIM
        )
        g_pair = lax.dynamic_slice_in_dim(grad_o, col_start, pair_cols, 1).reshape(
            block_rows, 2, HEAD_DIM
        )
        scores = (
            jnp.einsum("rhd,chd->hrc", q_pair, k_pair, preferred_element_type=jnp.float32) * factor
        )
        scores = scores.reshape(2, TILE_DEV, TILE, CANDT, TILE) + masking[None, :, None, :, None]
        scores = scores.reshape(2, block_rows, key_count)
        row_max = jnp.max(scores, axis=2, keepdims=True)
        exp_vals = jnp.exp(scores - row_max)
        prob_f32 = exp_vals / jnp.sum(exp_vals, axis=2, keepdims=True)
        prob_bf = prob_f32.astype(jnp.bfloat16)
        out_pair = jnp.einsum(
            "hrc,chd->rhd", prob_bf, v_pair, preferred_element_type=jnp.float32
        ).astype(jnp.bfloat16)
        grad_prob = jnp.einsum("rhd,chd->hrc", g_pair, v_pair, preferred_element_type=jnp.float32)
        row_delta = jnp.einsum(
            "rhd,rhd->hr", g_pair.astype(jnp.float32), out_pair.astype(jnp.float32)
        )
        grad_score = (prob_f32 * (grad_prob - row_delta[:, :, None]) * factor).astype(jnp.bfloat16)
        gq_pair = jnp.einsum(
            "hrc,chd->rhd", grad_score, k_pair, preferred_element_type=jnp.float32
        ).reshape(block_rows, pair_cols)
        gk_pair = jnp.einsum(
            "hrc,rhd->chd", grad_score, q_pair, preferred_element_type=jnp.float32
        ).reshape(key_count, pair_cols)
        gv_pair = jnp.einsum(
            "hrc,rhd->chd", prob_bf, g_pair, preferred_element_type=jnp.float32
        ).reshape(key_count, pair_cols)
        return (out_pair.reshape(block_rows, pair_cols), gq_pair, gk_pair, gv_pair)

    stacked = lax.map(head_pair, jnp.arange(HEADS // 2, dtype=jnp.int32))
    out_rows = joined(stacked[0], width_all)
    grad_q = joined(stacked[1], width_all)
    grad_k = joined(stacked[2], width_all)
    grad_v = joined(stacked[3], width_all)
    attended = jnp.dot(out_rows, w_out, preferred_element_type=jnp.float32).astype(jnp.bfloat16)
    grad_parts = jnp.concatenate([grad_k, grad_v], 1).reshape(3 + NB, block_rows, 2 * width_all)
    w_both32 = w_both.astype(jnp.float32)
    rows_f32 = node_rows.astype(jnp.float32)
    own_grad = returned_sum(grad_parts)
    kv_dx = jnp.dot(own_grad, w_both32.T, precision=highest)
    g_both = jnp.dot(rows_f32.T, own_grad, precision=highest)
    grad_x = jnp.dot(grad_q, w_query.astype(jnp.float32).T, precision=highest) + kv_dx
    g_query = jnp.dot(rows_f32.T, grad_q, precision=highest)
    g_out = jnp.dot(out_rows.T, cot_rows, preferred_element_type=jnp.float32)
    g_query, g_key, g_value, g_out = lax.psum(
        (g_query, g_both[:, :width_all], g_both[:, width_all:], g_out), ("dp", "dom")
    )
    return (attended[None], grad_x.astype(jnp.bfloat16)[None], g_query, g_key, g_value, g_out)


def solution(mesh):
    in_specs = (
        P("dp", "dom", None),
        P("dp", "dom", None),
        P("dp", "dom", None),
        P(),
        P(),
        P(),
        P(),
    )
    out_specs = (P("dp", "dom", None), P("dp", "dom", None), P(), P(), P(), P())
    return jax.shard_map(
        per_device, mesh=mesh, in_specs=in_specs, out_specs=out_specs, check_vma=False
    )
```

profile of v0, /device:TPU:8, one launch (start us, length us, event | category | flops | bytes accessed | tf_op | source)
XLA Modules:
  0.0 602.2 jit_solution(1646686012757670933)
XLA Ops:
  7.3 1.2 constant_dynamic-update-slice_fusion.5
  10.6 2.7 constant_dynamic-update-slice_fusion.11
  13.3 7.2 %collective-permute-start.4 = (bf16[384,1024]{1,0:T(8,128)(2,1)}, bf16[384,1024]{1,0:T(8,128)(2,1)S(1)}, u32[]{:S(2)}, u32[]{:S(2)}) collective-permute-start(bf16[384,1024]{1,0:T(8,128)(2,1)} %get-tuple-element.146), channel_id=1, source_target_pairs={{0,16},{1,17},{2,18},{3,19},{4,20},{5,21},{6,22},{7,23},{8,24},{9,... | collective-permute-start | bytes 2359304 | tf_op jit(solution)/shard_map/ppermute | solution.py:31
  21.0 2.6 collective-permute-start.2
  23.6 3.6 collective-permute-start.1
  28.1 45.5 %collective-permute-done = bf16[384,1024]{1,0:T(8,128)(2,1)} collective-permute-done((bf16[384,1024]{1,0:T(8,128)(2,1)}, bf16[384,1024]{1,0:T(8,128)(2,1)}, u32[]{:S(2)}, u32[]{:S(2)}) %collective-permute-start) | collective-permute-done | bytes 786464 | tf_op jit(solution)/shard_map/ppermute | solution.py:20
  73.5 2.1 constant_dynamic-update-slice_fusion.10
  75.7 2.1 constant_dynamic-update-slice_fusion.9
  77.8 2.1 constant_dynamic-update-slice_fusion.8
  79.8 2.1 constant_dynamic-update-slice_fusion.7
  82.8 4.8 fusion.33
  87.6 110.8 %while.16 = (s32[]{:T(128)}, bf16[4,384,128]{1,2,0:T(8,128)(2,1)}, f32[4,384,128]{1,2,0:T(8,128)}, f32[4,2304,128]{1,2,0:T(8,128)}, f32[4,2304,128]{1,2,0:T(8,12...) while((s32[]{:T(128)}, bf16[4,384,128]{1,2,0:T(8,128)(2,1)}, ...), condition=%wide.region_3.4_spmd, body=%wide.region_0.3_spmd.sunk | while | flops 1378665984 | bytes 104414744 | solution.py:121
  92.4 2.5 copy.50
  94.9 7.1 %fusion.93 = (f32[2,384]{1,0:T(2,128)S(1)}, f32[2,384,2304]{2,1,0:T(8,128)}) fusion(f32[384,2304]{1,0:T(8,128)} %bitcast.143, bf16[384,2,64]{0,2,1:T(8,128)(2,1)S(1)} %bitcast.150, bf16[2304,2,64]{0,2,1:T(8,128)(2,1)S(1)} %bitcast.144), kind=kOutput, calls=%fused_computation.74.clone.1 | convolution fusion | flops 233572608 | bytes 11308032 | tf_op jit(solution)/shard_map/while/body/eval_jaxpr/sub | solution.py:99
  102.0 3.8 fusion.94
  108.8 1.6 multiply_convert_fusion.2
  113.7 1.6 constant_dynamic-update-slice_fusion.17
  120.1 2.5 copy.50
  122.6 7.1 %fusion.93 = (f32[2,384]{1,0:T(2,128)S(1)}, f32[2,384,2304]{2,1,0:T(8,128)}) fusion(f32[384,2304]{1,0:T(8,128)} %bitcast.143, bf16[384,2,64]{0,2,1:T(8,128)(2,1)S(1)} %bitcast.150, bf16[2304,2,64]{0,2,1:T(8,128)(2,1)S(1)} %bitcast.144), kind=kOutput, calls=%fused_computation.74.clone.1 | convolution fusion | flops 233572608 | bytes 11308032 | tf_op jit(solution)/shard_map/while/body/eval_jaxpr/sub | solution.py:99
  129.7 3.8 fusion.94
  136.5 1.6 multiply_convert_fusion.2
  141.5 1.6 constant_dynamic-update-slice_fusion.17
  147.8 2.5 copy.50
  150.3 7.1 %fusion.93 = (f32[2,384]{1,0:T(2,128)S(1)}, f32[2,384,2304]{2,1,0:T(8,128)}) fusion(f32[384,2304]{1,0:T(8,128)} %bitcast.143, bf16[384,2,64]{0,2,1:T(8,128)(2,1)S(1)} %bitcast.150, bf16[2304,2,64]{0,2,1:T(8,128)(2,1)S(1)} %bitcast.144), kind=kOutput, calls=%fused_computation.74.clone.1 | convolution fusion | flops 233572608 | bytes 11308032 | tf_op jit(solution)/shard_map/while/body/eval_jaxpr/sub | solution.py:99
  157.4 3.8 fusion.94
  164.3 1.6 multiply_convert_fusion.2
  169.2 1.5 constant_dynamic-update-slice_fusion.17
  175.5 2.5 copy.50
  178.0 7.1 %fusion.93 = (f32[2,384]{1,0:T(2,128)S(1)}, f32[2,384,2304]{2,1,0:T(8,128)}) fusion(f32[384,2304]{1,0:T(8,128)} %bitcast.143, bf16[384,2,64]{0,2,1:T(8,128)(2,1)S(1)} %bitcast.150, bf16[2304,2,64]{0,2,1:T(8,128)(2,1)S(1)} %bitcast.144), kind=kOutput, calls=%fused_computation.74.clone.1 | convolution fusion | flops 233572608 | bytes 11308032 | tf_op jit(solution)/shard_map/while/body/eval_jaxpr/sub | solution.py:99
  185.1 3.8 fusion.94
  191.9 1.6 multiply_convert_fusion.2
  196.9 1.6 constant_dynamic-update-slice_fusion.17
  198.5 5.9 fusion.16
  204.4 6.2 %collective-permute-start.6 = (f32[384,1024]{0,1:T(8,128)}, f32[384,1024]{0,1:T(8,128)S(1)}, u32[]{:S(2)}, u32[]{:S(2)}) collective-permute-start(f32[384,1024]{0,1:T(8,128)} %get-tuple-element.137), channel_id=1, source_target_pairs={{1,0},{2,1},{3,2},{4,3},{5,4},{6,5},{7,6},{8,7},{9,8},{10,9},{11,1... | collective-permute-start | bytes 4718600 | tf_op jit(solution)/shard_map/ppermute | solution.py:23
  210.7 2.6 collective-permute-start.7
  213.2 4.3 collective-permute-start.9
  217.5 1.3 collective-permute-start.8
  218.9 1.4 fusion.23
  220.3 2.0 convolution_bitcast_fusion.1
  222.3 90.3 %collective-permute-done.5 = f32[384,1024]{0,1:T(8,128)S(1)} collective-permute-done((f32[384,1024]{0,1:T(8,128)}, f32[384,1024]{0,1:T(8,128)S(1)}, u32[]{:S(2)}, u32[]{:S(2)}) %collective-permute-start.5) | collective-permute-done | bytes 1572896 | tf_op jit(solution)/shard_map/ppermute | solution.py:20
  313.2 1.8 convolution_bitcast_fusion
  315.0 1.5 fusion.34
  317.7 2.7 fusion.38
  320.4 3.4 fusion.21
  323.8 264.0 %all-reduce.3.cloned.1.call-done = (f32[512,512]{0,1:T(8,128)}, f32[512,512]{0,1:T(8,128)}, f32[512,512]{0,1:T(8,128)}, f32[512,512]{1,0:T(8,128)}) async-done(((f32[512,512]{0,1:T(8,128)}, f32[512,512]{0,1:T(8,128)}, f32[512,512]{0,1:T(8,128)}, f32[512,512]{1,0:T(8,128)}), (f32[512,512]{0,1:T(8,128)}, f32[512,512]{0,1:T(8,128)}, f32[512,512]{0,1:T(8,128)}, ...) | async-done | bytes 4194320 | tf_op jit(solution)/shard_map/psum | solution.py:136
  587.9 2.7 copy.24
  590.5 2.5 copy.25
  593.1 1.3 copy.26
  (149 shorter events, 48.2 us)
Async XLA Ops:
  7.2 20.5 %copy-start = (bf16[512,512]{1,0:T(8,128)(2,1)S(1)}, bf16[512,512]{1,0:T(8,128)(2,1)}, u32[]{:S(2)}) copy-start(bf16[512,512]{1,0:T(8,128)(2,1)} %param.15) | copy-start | bytes 1572868
  7.2 20.0 %copy-start.4 = (bf16[1,384,512]{2,1,0:T(8,128)(2,1)S(1)}, bf16[1,384,512]{2,1,0:T(8,128)(2,1)}, u32[]{:S(2)}) copy-start(bf16[1,384,512]{2,1,0:T(8,128)(2,1)} %param.9) | copy-start | bytes 1179652
  7.2 20.0 %copy-start.6 = (bf16[512,512]{1,0:T(8,128)(2,1)S(1)}, bf16[512,512]{1,0:T(8,128)(2,1)}, u32[]{:S(2)}) copy-start(bf16[512,512]{1,0:T(8,128)(2,1)} %param.12) | copy-start | bytes 1572868
  7.2 20.4 %copy-start.14 = (s32[1,3,18]{2,0,1:T(1,128)S(1)}, s32[1,3,18]{2,0,1:T(1,128)}, u32[]{:S(2)}) copy-start(s32[1,3,18]{2,0,1:T(1,128)} %param.10) | copy-start | bytes 652
  7.2 20.4 %copy-start.9 = (bf16[1,384,512]{2,1,0:T(8,128)(2,1)S(1)}, bf16[1,384,512]{2,1,0:T(8,128)(2,1)}, u32[]{:S(2)}) copy-start(bf16[1,384,512]{2,1,0:T(8,128)(2,1)} %param.11) | copy-start | bytes 1179652
  7.2 580.6 %all-reduce.3.cloned.1.call-start = ((), (), s32[]{:S(2)}) async-start(), calls=%async_computation | async-start | bytes 8388608 | tf_op jit(solution)/shard_map/psum | solution.py:136
  9.6 1.0 copy-start.2
  13.3 68.6 %collective-permute-start.4 = (bf16[384,1024]{1,0:T(8,128)(2,1)}, bf16[384,1024]{1,0:T(8,128)(2,1)S(1)}, u32[]{:S(2)}, u32[]{:S(2)}) collective-permute-start(bf16[384,1024]{1,0:T(8,128)(2,1)} %get-tuple-element.146), channel_id=1, source_target_pairs={{0,16},{1,17},{2,18},{3,19},{4,20},{5,21},{6,22},{7,23},{8,24},{9,... | collective-permute-start | bytes 2359304 | tf_op jit(solution)/shard_map/ppermute | solution.py:31
  20.5 59.3 %collective-permute-start.3 = (bf16[384,1024]{1,0:T(8,128)(2,1)}, bf16[384,1024]{1,0:T(8,128)(2,1)}, u32[]{:S(2)}, u32[]{:S(2)}) collective-permute-start(bf16[384,1024]{1,0:T(8,128)(2,1)} %get-tuple-element.146), channel_id=1, source_target_pairs={{0,32},{1,33},{2,34},{3,35},{4,36},{5,37},{6,38},{7,39},{8,40},{9,... | collective-permute-start | bytes 2359304 | tf_op jit(solution)/shard_map/ppermute | solution.py:31
  21.0 56.8 %collective-permute-start.2 = (bf16[384,1024]{1,0:T(8,128)(2,1)}, bf16[384,1024]{1,0:T(8,128)(2,1)}, u32[]{:S(2)}, u32[]{:S(2)}) collective-permute-start(bf16[384,1024]{1,0:T(8,128)(2,1)} %get-tuple-element.146), channel_id=1, source_target_pairs={{0,64},{1,65},{2,66},{3,67},{4,68},{5,69},{6,70},{7,71},{8,72},{9,... | collective-permute-start | bytes 2359304 | tf_op jit(solution)/shard_map/ppermute | solution.py:31
  23.6 52.1 %collective-permute-start.1 = (bf16[384,1024]{1,0:T(8,128)(2,1)}, bf16[384,1024]{1,0:T(8,128)(2,1)}, u32[]{:S(2)}, u32[]{:S(2)}) collective-permute-start(bf16[384,1024]{1,0:T(8,128)(2,1)} %get-tuple-element.146), channel_id=1, source_target_pairs={{1,0},{2,1},{3,2},{4,3},{5,4},{6,5},{7,6},{8,7},{9,8},{10,9},{11,1... | collective-permute-start | bytes 2359304 | tf_op jit(solution)/shard_map/ppermute | solution.py:23
  27.2 46.4 %collective-permute-start = (bf16[384,1024]{1,0:T(8,128)(2,1)}, bf16[384,1024]{1,0:T(8,128)(2,1)}, u32[]{:S(2)}, u32[]{:S(2)}) collective-permute-start(bf16[384,1024]{1,0:T(8,128)(2,1)} %get-tuple-element.146), channel_id=1, source_target_pairs={{0,1},{1,2},{2,3},{3,4},{4,5},{5,6},{6,7},{7,8},{8,9},{9,10},{10,1... | collective-permute-start | bytes 2359304 | tf_op jit(solution)/shard_map/ppermute | solution.py:20
  87.6 1.5 copy-start.7
  105.8 3.0 copy-start.1
  112.4 3.0 copy-start.8
  115.4 1.5 copy-start.7
  133.5 3.0 copy-start.1
  140.1 3.0 copy-start.8
  143.1 1.5 copy-start.7
  161.3 3.0 copy-start.1
  167.8 2.9 copy-start.8
  170.8 1.5 copy-start.7
  188.9 3.0 copy-start.1
  195.5 2.9 copy-start.8
  198.4 114.2 %slice-start = ((s8[4718592]{0:T(1024)(128)(4,1)}), s8[4194304]{0:T(1024)(128)(4,1)S(1)}, s32[]{:S(2)}) async-start(s8[4718592]{0:T(1024)(128)(4,1)} %bitcast.156), calls=%async_computation.1 | async-start | bytes 8388608
  198.4 114.2 %slice-start.2 = ((s8[4718592]{0:T(1024)(128)(4,1)}), s8[4194304]{0:T(1024)(128)(4,1)S(1)}, s32[]{:S(2)}) async-start(s8[4718592]{0:T(1024)(128)(4,1)} %bitcast.160), calls=%async_computation.3 | async-start | bytes 8388608
  198.4 20.5 %copy-start.10 = (bf16[1,384,512]{2,1,0:T(8,128)(2,1)S(1)}, bf16[1,384,512]{2,1,0:T(8,128)(2,1)}, u32[]{:S(2)}) copy-start(bf16[1,384,512]{2,1,0:T(8,128)(2,1)} %param.11) | copy-start | bytes 1179652
  198.4 20.5 %copy-start.11 = (bf16[4,384,128]{1,2,0:T(8,128)(2,1)S(1)}, bf16[4,384,128]{1,2,0:T(8,128)(2,1)}, u32[]{:S(2)}) copy-start(bf16[4,384,128]{1,2,0:T(8,128)(2,1)} %get-tuple-element.66) | copy-start | bytes 1179652
  198.4 21.9 %copy-start.5 = (f32[4,384,128]{1,2,0:T(8,128)S(1)}, f32[4,384,128]{1,2,0:T(8,128)}, u32[]{:S(2)}) copy-start(f32[4,384,128]{1,2,0:T(8,128)} %get-tuple-element.67) | copy-start | bytes 2359300
  198.5 114.2 %slice-start.1 = ((s8[4718592]{0:T(1024)(128)(4,1)}), s8[524288]{0:T(1024)(128)(4,1)S(1)}, s32[]{:S(2)}) async-start(s8[4718592]{0:T(1024)(128)(4,1)} %bitcast.156), calls=%async_computation.2 | async-start | bytes 1048576
  198.5 114.2 %slice-start.3 = ((s8[4718592]{0:T(1024)(128)(4,1)}), s8[524288]{0:T(1024)(128)(4,1)S(1)}, s32[]{:S(2)}) async-start(s8[4718592]{0:T(1024)(128)(4,1)} %bitcast.160), calls=%async_computation.4 | async-start | bytes 1048576
  204.4 108.2 %collective-permute-start.5 = (f32[384,1024]{0,1:T(8,128)}, f32[384,1024]{0,1:T(8,128)S(1)}, u32[]{:S(2)}, u32[]{:S(2)}) collective-permute-start(f32[384,1024]{0,1:T(8,128)} %get-tuple-element.136), channel_id=1, source_target_pairs={{0,1},{1,2},{2,3},{3,4},{4,5},{5,6},{6,7},{7,8},{8,9},{9,10},{10,1... | collective-permute-start | bytes 4718600 | tf_op jit(solution)/shard_map/ppermute | solution.py:20
  204.4 108.2 %collective-permute-start.6 = (f32[384,1024]{0,1:T(8,128)}, f32[384,1024]{0,1:T(8,128)S(1)}, u32[]{:S(2)}, u32[]{:S(2)}) collective-permute-start(f32[384,1024]{0,1:T(8,128)} %get-tuple-element.137), channel_id=1, source_target_pairs={{1,0},{2,1},{3,2},{4,3},{5,4},{6,5},{7,6},{8,7},{9,8},{10,9},{11,1... | collective-permute-start | bytes 4718600 | tf_op jit(solution)/shard_map/ppermute | solution.py:23
  210.7 102.0 %collective-permute-start.7 = (f32[384,1024]{0,1:T(8,128)}, f32[384,1024]{0,1:T(8,128)S(1)}, u32[]{:S(2)}, u32[]{:S(2)}) collective-permute-start(f32[384,1024]{0,1:T(8,128)} %get-tuple-element.138), channel_id=1, source_target_pairs={{0,64},{1,65},{2,66},{3,67},{4,68},{5,69},{6,70},{7,71},{8,72},{9,... | collective-permute-start | bytes 4718600 | tf_op jit(solution)/shard_map/ppermute | solution.py:31
  213.2 99.4 %collective-permute-start.9 = (f32[384,1024]{0,1:T(8,128)S(1)}, f32[384,1024]{0,1:T(8,128)S(1)}, u32[]{:S(2)}, u32[]{:S(2)}) collective-permute-start(f32[384,1024]{0,1:T(8,128)S(1)} %get-tuple-element.139), channel_id=1, source_target_pairs={{0,16},{1,17},{2,18},{3,19},{4,20},{5,21},{6,22},{7,23},{8,24},{9,... | collective-permute-start | bytes 4718600 | tf_op jit(solution)/shard_map/ppermute | solution.py:31
  217.5 95.1 %collective-permute-start.8 = (f32[384,1024]{0,1:T(8,128)S(1)}, f32[384,1024]{0,1:T(8,128)S(1)}, u32[]{:S(2)}, u32[]{:S(2)}) collective-permute-start(f32[384,1024]{0,1:T(8,128)S(1)} %get-tuple-element.140), channel_id=1, source_target_pairs={{0,32},{1,33},{2,34},{3,35},{4,36},{5,37},{6,38},{7,39},{8,40},{9,... | collective-permute-start | bytes 4718600 | tf_op jit(solution)/shard_map/ppermute | solution.py:31
  316.5 3.9 copy-start.3
  587.9 5.2 copy-start.13
  587.9 6.5 %copy-start.12 = (f32[512,512]{1,0:T(8,128)S(1)}, f32[512,512]{1,0:T(8,128)}, u32[]{:S(2)}) copy-start(f32[512,512]{1,0:T(8,128)} %get-tuple-element.276) | copy-start | bytes 3145732
Sparse Core Ops, SparseCore 0:
  316.7 271.1 all-reduce.2
where the time goes:
time: 603 us; the launch traced here: 602 us
  waiting for transfers between devices  400 us (66%)
  local copies, waits for them, and re-layouts  68.6 us (11%)
  matrix products  66.2 us (11%)
  starting transfers between devices  28.4 us (5%)
  other arithmetic  21.8 us (4%)
  between operations  14.3 us (2%)
    psum x1, waiting for transfers between devices, per_device(): lax.psum((g_query, g_both[:, :width_all], g_both[:, width_all:], g_out),...  264 us
    ppermute x2, waiting for transfers between devices, with_halo(): lax.ppermute(lax.slice_in_dim(block, block.shape[dim] - width, None, axis...  136 us
    sub x4, matrix products, head_pair(): exp_vals = jnp.exp(scores - row_max)  28.3 us
    ppermute x6, starting transfers between devices, from_partner(): return lax.ppermute(value, axis, pairs)  18.5 us
    unnamed x41, local copies, waits for them, and re-layouts  18.1 us
    convert_element_type x4, other arithmetic, head_pair(): prob_bf = prob_f32.astype(jnp.bfloat16)  15.3 us
    while x28, local copies, waits for them, and re-layouts  14.3 us
  transfers between devices with their start and end apart: 11, of which 3 were waited for; matrix products, arithmetic and copies ran while one was open for 3% of the time, Pallas kernels for 0%

commit v1 on v0

--- a/solution.py
+++ b/solution.py
@@ -134,7 +134,7 @@
     g_query = jnp.dot(rows_f32.T, grad_q, precision=highest)
     g_out = jnp.dot(out_rows.T, cot_rows, preferred_element_type=jnp.float32)
     g_query, g_key, g_value, g_out = lax.psum(
-        (g_query, g_both[:, :width_all], g_both[:, width_all:], g_out), ("dp", "dom")
+        lax.psum((g_query, g_both[:, :width_all], g_both[:, width_all:], g_out), "dp"), "dom"
     )
     return (attended[None], grad_x.astype(jnp.bfloat16)[None], g_query, g_key, g_value, g_out)
 

time: 603 us -> 617 us (1.023)
  waiting for transfers between devices: 400 us -> 413 us
    psum x0 -> x1, waiting for transfers between devices: none -> 236 us  [per_device(): lax.psum(lax.psum((g_query, g_both[:, :width_all], g_both[:, width_all:],...]
    psum x1, waiting for transfers between devices: 264 us -> 41 us  [per_device(): lax.psum((g_query, g_both[:, :width_all], g_both[:, width_all:], g_out),...]
  transfers between devices with their start and end apart: 11 -> 12, of which waited for: 3 -> 4; matrix products, arithmetic and copies ran while one was open for 3% -> 3% of each run, Pallas kernels for 0% -> 0%
where the time goes in v1:
time: 617 us; the launch traced here: 615 us
  waiting for transfers between devices  413 us (67%)
  local copies, waits for them, and re-layouts  68.5 us (11%)
  matrix products  66.2 us (11%)
  starting transfers between devices  28.4 us (5%)
  other arithmetic  21.8 us (4%)
  between operations  14.3 us (2%)
    psum x1, waiting for transfers between devices, per_device(): lax.psum(lax.psum((g_query, g_both[:, :width_all], g_both[:, width_all:],...  236 us
    ppermute x2, waiting for transfers between devices, with_halo(): lax.ppermute(lax.slice_in_dim(block, block.shape[dim] - width, None, axis...  136 us
    psum x1, waiting for transfers between devices, per_device(): lax.psum((g_query, g_both[:, :width_all], g_both[:, width_all:], g_out),...  41 us
    sub x4, matrix products, head_pair(): exp_vals = jnp.exp(scores - row_max)  28.4 us
    ppermute x6, starting transfers between devices, from_partner(): return lax.ppermute(value, axis, pairs)  18.5 us
    unnamed x41, local copies, waits for them, and re-layouts  18 us
    convert_element_type x4, other arithmetic, head_pair(): prob_bf = prob_f32.astype(jnp.bfloat16)  15.3 us
    while x28, local copies, waits for them, and re-layouts  14.3 us
  transfers between devices with their start and end apart: 12, of which 4 were waited for; matrix products, arithmetic and copies ran while one was open for 3% of the time, Pallas kernels for 0%

profile of v1, /device:TPU:8, one launch (start us, length us, event | category | flops | bytes accessed | tf_op | source)
XLA Modules:
  0.0 615.2 jit_solution(12341521339595849086)
XLA Ops:
  10.6 2.7 constant_dynamic-update-slice_fusion.11
  13.3 7.2 %collective-permute-start.4 = (bf16[384,1024]{1,0:T(8,128)(2,1)}, bf16[384,1024]{1,0:T(8,128)(2,1)S(1)}, u32[]{:S(2)}, u32[]{:S(2)}) collective-permute-start(bf16[384,1024]{1,0:T(8,128)(2,1)} %get-tuple-element.150), channel_id=1, source_target_pairs={{0,16},{1,17},{2,18},{3,19},{4,20},{5,21},{6,22},{7,23},{8,24},{9,... | collective-permute-start | bytes 2359304 | tf_op jit(solution)/shard_map/ppermute | solution.py:31
  21.0 2.6 collective-permute-start.2
  23.5 3.6 collective-permute-start.1
  28.1 45.5 %collective-permute-done = bf16[384,1024]{1,0:T(8,128)(2,1)} collective-permute-done((bf16[384,1024]{1,0:T(8,128)(2,1)}, bf16[384,1024]{1,0:T(8,128)(2,1)}, u32[]{:S(2)}, u32[]{:S(2)}) %collective-permute-start) | collective-permute-done | bytes 786464 | tf_op jit(solution)/shard_map/ppermute | solution.py:20
  73.5 2.1 constant_dynamic-update-slice_fusion.10
  75.6 2.1 constant_dynamic-update-slice_fusion.9
  77.7 2.1 constant_dynamic-update-slice_fusion.8
  79.8 2.1 constant_dynamic-update-slice_fusion.7
  82.8 4.8 fusion.33
  87.6 110.8 %while.16 = (s32[]{:T(128)}, bf16[4,384,128]{1,2,0:T(8,128)(2,1)}, f32[4,384,128]{1,2,0:T(8,128)}, f32[4,2304,128]{1,2,0:T(8,128)}, f32[4,2304,128]{1,2,0:T(8,12...) while((s32[]{:T(128)}, bf16[4,384,128]{1,2,0:T(8,128)(2,1)}, ...), condition=%wide.region_3.4_spmd, body=%wide.region_0.3_spmd.sunk | while | flops 1378665984 | bytes 104414744 | solution.py:121
  92.3 2.5 copy.50
  94.8 7.1 %fusion.93 = (f32[2,384]{1,0:T(2,128)S(1)}, f32[2,384,2304]{2,1,0:T(8,128)}) fusion(f32[384,2304]{1,0:T(8,128)} %bitcast.143, bf16[384,2,64]{0,2,1:T(8,128)(2,1)S(1)} %bitcast.150, bf16[2304,2,64]{0,2,1:T(8,128)(2,1)S(1)} %bitcast.144), kind=kOutput, calls=%fused_computation.74.clone.1 | convolution fusion | flops 233572608 | bytes 11308032 | tf_op jit(solution)/shard_map/while/body/eval_jaxpr/sub | solution.py:99
  101.9 3.8 fusion.94
  108.7 1.6 multiply_convert_fusion.2
  113.7 1.7 constant_dynamic-update-slice_fusion.17
  120.1 2.5 copy.50
  122.6 7.1 %fusion.93 = (f32[2,384]{1,0:T(2,128)S(1)}, f32[2,384,2304]{2,1,0:T(8,128)}) fusion(f32[384,2304]{1,0:T(8,128)} %bitcast.143, bf16[384,2,64]{0,2,1:T(8,128)(2,1)S(1)} %bitcast.150, bf16[2304,2,64]{0,2,1:T(8,128)(2,1)S(1)} %bitcast.144), kind=kOutput, calls=%fused_computation.74.clone.1 | convolution fusion | flops 233572608 | bytes 11308032 | tf_op jit(solution)/shard_map/while/body/eval_jaxpr/sub | solution.py:99
  129.7 3.8 fusion.94
  136.5 1.6 multiply_convert_fusion.2
  141.5 1.6 constant_dynamic-update-slice_fusion.17
  147.8 2.5 copy.50
  150.3 7.1 %fusion.93 = (f32[2,384]{1,0:T(2,128)S(1)}, f32[2,384,2304]{2,1,0:T(8,128)}) fusion(f32[384,2304]{1,0:T(8,128)} %bitcast.143, bf16[384,2,64]{0,2,1:T(8,128)(2,1)S(1)} %bitcast.150, bf16[2304,2,64]{0,2,1:T(8,128)(2,1)S(1)} %bitcast.144), kind=kOutput, calls=%fused_computation.74.clone.1 | convolution fusion | flops 233572608 | bytes 11308032 | tf_op jit(solution)/shard_map/while/body/eval_jaxpr/sub | solution.py:99
  157.4 3.8 fusion.94
  164.3 1.6 multiply_convert_fusion.2
  169.2 1.6 constant_dynamic-update-slice_fusion.17
  175.5 2.5 copy.50
  178.0 7.1 %fusion.93 = (f32[2,384]{1,0:T(2,128)S(1)}, f32[2,384,2304]{2,1,0:T(8,128)}) fusion(f32[384,2304]{1,0:T(8,128)} %bitcast.143, bf16[384,2,64]{0,2,1:T(8,128)(2,1)S(1)} %bitcast.150, bf16[2304,2,64]{0,2,1:T(8,128)(2,1)S(1)} %bitcast.144), kind=kOutput, calls=%fused_computation.74.clone.1 | convolution fusion | flops 233572608 | bytes 11308032 | tf_op jit(solution)/shard_map/while/body/eval_jaxpr/sub | solution.py:99
  185.1 3.8 fusion.94
  191.9 1.6 multiply_convert_fusion.2
  196.9 1.5 constant_dynamic-update-slice_fusion.17
  198.5 5.9 fusion.16
  204.4 6.2 %collective-permute-start.6 = (f32[384,1024]{0,1:T(8,128)}, f32[384,1024]{0,1:T(8,128)S(1)}, u32[]{:S(2)}, u32[]{:S(2)}) collective-permute-start(f32[384,1024]{0,1:T(8,128)} %get-tuple-element.141), channel_id=1, source_target_pairs={{1,0},{2,1},{3,2},{4,3},{5,4},{6,5},{7,6},{8,7},{9,8},{10,9},{11,1... | collective-permute-start | bytes 4718600 | tf_op jit(solution)/shard_map/ppermute | solution.py:23
  210.6 2.6 collective-permute-start.7
  213.2 4.3 collective-permute-start.9
  217.6 1.3 collective-permute-start.8
  218.9 1.5 fusion.23
  220.4 2.0 convolution_bitcast_fusion.1
  222.3 90.3 %collective-permute-done.5 = f32[384,1024]{0,1:T(8,128)S(1)} collective-permute-done((f32[384,1024]{0,1:T(8,128)}, f32[384,1024]{0,1:T(8,128)S(1)}, u32[]{:S(2)}, u32[]{:S(2)}) %collective-permute-start.5) | collective-permute-done | bytes 1572896 | tf_op jit(solution)/shard_map/ppermute | solution.py:20
  313.2 1.8 convolution_bitcast_fusion
  315.1 1.5 fusion.34
  316.6 41.0 %all-reduce.7.cloned.1.call-done = (f32[512,512]{0,1:T(8,128)}, f32[512,512]{0,1:T(8,128)}, f32[512,512]{0,1:T(8,128)}, f32[512,512]{1,0:T(8,128)}) async-done(((f32[512,512]{0,1:T(8,128)}, f32[512,512]{0,1:T(8,128)}, f32[512,512]{0,1:T(8,128)}, f32[512,512]{1,0:T(8,128)}), (f32[512,512]{0,1:T(8,128)}, f32[512,512]{0,1:T(8,128)}, f32[512,512]{0,1:T(8,128)}, ...) | async-done | bytes 4194320 | tf_op jit(solution)/shard_map/psum | solution.py:137
  358.8 2.7 fusion.38
  361.6 3.4 fusion.21
  365.0 235.9 %all-reduce.5.cloned.1.call-done = (f32[512,512]{0,1:T(8,128)}, f32[512,512]{0,1:T(8,128)}, f32[512,512]{0,1:T(8,128)}, f32[512,512]{1,0:T(8,128)}) async-done(((f32[512,512]{0,1:T(8,128)}, f32[512,512]{0,1:T(8,128)}, f32[512,512]{0,1:T(8,128)}, f32[512,512]{1,0:T(8,128)}), (f32[512,512]{0,1:T(8,128)}, f32[512,512]{0,1:T(8,128)}, f32[512,512]{0,1:T(8,128)}, ...) | async-done | bytes 4194320 | tf_op jit(solution)/shard_map/psum | solution.py:136
  600.9 2.7 copy.24
  603.6 2.5 copy.25
  606.1 1.3 copy.26
  (152 shorter events, 49.4 us)
Async XLA Ops:
  7.2 20.5 %copy-start = (bf16[512,512]{1,0:T(8,128)(2,1)S(1)}, bf16[512,512]{1,0:T(8,128)(2,1)}, u32[]{:S(2)}) copy-start(bf16[512,512]{1,0:T(8,128)(2,1)} %param.15) | copy-start | bytes 1572868
  7.2 20.0 %copy-start.4 = (bf16[1,384,512]{2,1,0:T(8,128)(2,1)S(1)}, bf16[1,384,512]{2,1,0:T(8,128)(2,1)}, u32[]{:S(2)}) copy-start(bf16[1,384,512]{2,1,0:T(8,128)(2,1)} %param.9) | copy-start | bytes 1179652
  7.2 20.0 %copy-start.6 = (bf16[512,512]{1,0:T(8,128)(2,1)S(1)}, bf16[512,512]{1,0:T(8,128)(2,1)}, u32[]{:S(2)}) copy-start(bf16[512,512]{1,0:T(8,128)(2,1)} %param.12) | copy-start | bytes 1572868
  7.2 20.4 %copy-start.14 = (s32[1,3,18]{2,0,1:T(1,128)S(1)}, s32[1,3,18]{2,0,1:T(1,128)}, u32[]{:S(2)}) copy-start(s32[1,3,18]{2,0,1:T(1,128)} %param.10) | copy-start | bytes 652
  7.2 20.4 %copy-start.9 = (bf16[1,384,512]{2,1,0:T(8,128)(2,1)S(1)}, bf16[1,384,512]{2,1,0:T(8,128)(2,1)}, u32[]{:S(2)}) copy-start(bf16[1,384,512]{2,1,0:T(8,128)(2,1)} %param.11) | copy-start | bytes 1179652
  7.2 350.4 %all-reduce.7.cloned.1.call-start = ((), (), s32[]{:S(2)}) async-start(), calls=%async_computation.1 | async-start | bytes 8388608 | tf_op jit(solution)/shard_map/psum | solution.py:137
  9.6 1.0 copy-start.2
  13.3 68.5 %collective-permute-start.4 = (bf16[384,1024]{1,0:T(8,128)(2,1)}, bf16[384,1024]{1,0:T(8,128)(2,1)S(1)}, u32[]{:S(2)}, u32[]{:S(2)}) collective-permute-start(bf16[384,1024]{1,0:T(8,128)(2,1)} %get-tuple-element.150), channel_id=1, source_target_pairs={{0,16},{1,17},{2,18},{3,19},{4,20},{5,21},{6,22},{7,23},{8,24},{9,... | collective-permute-start | bytes 2359304 | tf_op jit(solution)/shard_map/ppermute | solution.py:31
  20.5 59.3 %collective-permute-start.3 = (bf16[384,1024]{1,0:T(8,128)(2,1)}, bf16[384,1024]{1,0:T(8,128)(2,1)}, u32[]{:S(2)}, u32[]{:S(2)}) collective-permute-start(bf16[384,1024]{1,0:T(8,128)(2,1)} %get-tuple-element.150), channel_id=1, source_target_pairs={{0,32},{1,33},{2,34},{3,35},{4,36},{5,37},{6,38},{7,39},{8,40},{9,... | collective-permute-start | bytes 2359304 | tf_op jit(solution)/shard_map/ppermute | solution.py:31
  21.0 56.7 %collective-permute-start.2 = (bf16[384,1024]{1,0:T(8,128)(2,1)}, bf16[384,1024]{1,0:T(8,128)(2,1)}, u32[]{:S(2)}, u32[]{:S(2)}) collective-permute-start(bf16[384,1024]{1,0:T(8,128)(2,1)} %get-tuple-element.150), channel_id=1, source_target_pairs={{0,64},{1,65},{2,66},{3,67},{4,68},{5,69},{6,70},{7,71},{8,72},{9,... | collective-permute-start | bytes 2359304 | tf_op jit(solution)/shard_map/ppermute | solution.py:31
  23.5 52.1 %collective-permute-start.1 = (bf16[384,1024]{1,0:T(8,128)(2,1)}, bf16[384,1024]{1,0:T(8,128)(2,1)}, u32[]{:S(2)}, u32[]{:S(2)}) collective-permute-start(bf16[384,1024]{1,0:T(8,128)(2,1)} %get-tuple-element.150), channel_id=1, source_target_pairs={{1,0},{2,1},{3,2},{4,3},{5,4},{6,5},{7,6},{8,7},{9,8},{10,9},{11,1... | collective-permute-start | bytes 2359304 | tf_op jit(solution)/shard_map/ppermute | solution.py:23
  27.2 46.4 %collective-permute-start = (bf16[384,1024]{1,0:T(8,128)(2,1)}, bf16[384,1024]{1,0:T(8,128)(2,1)}, u32[]{:S(2)}, u32[]{:S(2)}) collective-permute-start(bf16[384,1024]{1,0:T(8,128)(2,1)} %get-tuple-element.150), channel_id=1, source_target_pairs={{0,1},{1,2},{2,3},{3,4},{4,5},{5,6},{6,7},{7,8},{8,9},{9,10},{10,1... | collective-permute-start | bytes 2359304 | tf_op jit(solution)/shard_map/ppermute | solution.py:20
  87.6 1.5 copy-start.7
  105.7 3.0 copy-start.1
  112.3 3.0 copy-start.8
  115.3 1.5 copy-start.7
  133.5 3.0 copy-start.1
  140.1 3.0 copy-start.8
  143.1 1.5 copy-start.7
  161.2 3.0 copy-start.1
  167.8 2.9 copy-start.8
  170.8 1.5 copy-start.7
  188.9 3.0 copy-start.1
  195.5 2.9 copy-start.8
  198.4 114.3 %slice-start = ((s8[4718592]{0:T(1024)(128)(4,1)}), s8[4194304]{0:T(1024)(128)(4,1)S(1)}, s32[]{:S(2)}) async-start(s8[4718592]{0:T(1024)(128)(4,1)} %bitcast.156), calls=%async_computation.2 | async-start | bytes 8388608
  198.4 114.3 %slice-start.2 = ((s8[4718592]{0:T(1024)(128)(4,1)}), s8[4194304]{0:T(1024)(128)(4,1)S(1)}, s32[]{:S(2)}) async-start(s8[4718592]{0:T(1024)(128)(4,1)} %bitcast.160), calls=%async_computation.4 | async-start | bytes 8388608
  198.4 20.5 %copy-start.10 = (bf16[1,384,512]{2,1,0:T(8,128)(2,1)S(1)}, bf16[1,384,512]{2,1,0:T(8,128)(2,1)}, u32[]{:S(2)}) copy-start(bf16[1,384,512]{2,1,0:T(8,128)(2,1)} %param.11) | copy-start | bytes 1179652
  198.4 20.5 %copy-start.11 = (bf16[4,384,128]{1,2,0:T(8,128)(2,1)S(1)}, bf16[4,384,128]{1,2,0:T(8,128)(2,1)}, u32[]{:S(2)}) copy-start(bf16[4,384,128]{1,2,0:T(8,128)(2,1)} %get-tuple-element.66) | copy-start | bytes 1179652
  198.4 21.9 %copy-start.5 = (f32[4,384,128]{1,2,0:T(8,128)S(1)}, f32[4,384,128]{1,2,0:T(8,128)}, u32[]{:S(2)}) copy-start(f32[4,384,128]{1,2,0:T(8,128)} %get-tuple-element.67) | copy-start | bytes 2359300
  198.4 114.2 %slice-start.1 = ((s8[4718592]{0:T(1024)(128)(4,1)}), s8[524288]{0:T(1024)(128)(4,1)S(1)}, s32[]{:S(2)}) async-start(s8[4718592]{0:T(1024)(128)(4,1)} %bitcast.156), calls=%async_computation.3 | async-start | bytes 1048576
  198.4 114.2 %slice-start.3 = ((s8[4718592]{0:T(1024)(128)(4,1)}), s8[524288]{0:T(1024)(128)(4,1)S(1)}, s32[]{:S(2)}) async-start(s8[4718592]{0:T(1024)(128)(4,1)} %bitcast.160), calls=%async_computation.5 | async-start | bytes 1048576
  204.4 108.2 %collective-permute-start.5 = (f32[384,1024]{0,1:T(8,128)}, f32[384,1024]{0,1:T(8,128)S(1)}, u32[]{:S(2)}, u32[]{:S(2)}) collective-permute-start(f32[384,1024]{0,1:T(8,128)} %get-tuple-element.140), channel_id=1, source_target_pairs={{0,1},{1,2},{2,3},{3,4},{4,5},{5,6},{6,7},{7,8},{8,9},{9,10},{10,1... | collective-permute-start | bytes 4718600 | tf_op jit(solution)/shard_map/ppermute | solution.py:20
  204.4 108.2 %collective-permute-start.6 = (f32[384,1024]{0,1:T(8,128)}, f32[384,1024]{0,1:T(8,128)S(1)}, u32[]{:S(2)}, u32[]{:S(2)}) collective-permute-start(f32[384,1024]{0,1:T(8,128)} %get-tuple-element.141), channel_id=1, source_target_pairs={{1,0},{2,1},{3,2},{4,3},{5,4},{6,5},{7,6},{8,7},{9,8},{10,9},{11,1... | collective-permute-start | bytes 4718600 | tf_op jit(solution)/shard_map/ppermute | solution.py:23
  210.6 102.0 %collective-permute-start.7 = (f32[384,1024]{0,1:T(8,128)}, f32[384,1024]{0,1:T(8,128)S(1)}, u32[]{:S(2)}, u32[]{:S(2)}) collective-permute-start(f32[384,1024]{0,1:T(8,128)} %get-tuple-element.142), channel_id=1, source_target_pairs={{0,64},{1,65},{2,66},{3,67},{4,68},{5,69},{6,70},{7,71},{8,72},{9,... | collective-permute-start | bytes 4718600 | tf_op jit(solution)/shard_map/ppermute | solution.py:31
  213.2 99.4 %collective-permute-start.9 = (f32[384,1024]{0,1:T(8,128)S(1)}, f32[384,1024]{0,1:T(8,128)S(1)}, u32[]{:S(2)}, u32[]{:S(2)}) collective-permute-start(f32[384,1024]{0,1:T(8,128)S(1)} %get-tuple-element.143), channel_id=1, source_target_pairs={{0,16},{1,17},{2,18},{3,19},{4,20},{5,21},{6,22},{7,23},{8,24},{9,... | collective-permute-start | bytes 4718600 | tf_op jit(solution)/shard_map/ppermute | solution.py:31
  217.6 95.1 %collective-permute-start.8 = (f32[384,1024]{0,1:T(8,128)S(1)}, f32[384,1024]{0,1:T(8,128)S(1)}, u32[]{:S(2)}, u32[]{:S(2)}) collective-permute-start(f32[384,1024]{0,1:T(8,128)S(1)} %get-tuple-element.144), channel_id=1, source_target_pairs={{0,32},{1,33},{2,34},{3,35},{4,36},{5,37},{6,38},{7,39},{8,40},{9,... | collective-permute-start | bytes 4718600 | tf_op jit(solution)/shard_map/ppermute | solution.py:31
  316.6 284.3 %all-reduce.5.cloned.1.call-start = ((), (), s32[]{:S(2)}) async-start(), calls=%async_computation | async-start | bytes 8388608 | tf_op jit(solution)/shard_map/psum | solution.py:136
  357.7 3.9 copy-start.3
  600.9 5.2 copy-start.13
  600.9 6.5 %copy-start.12 = (f32[512,512]{1,0:T(8,128)S(1)}, f32[512,512]{1,0:T(8,128)}, u32[]{:S(2)}) copy-start(f32[512,512]{1,0:T(8,128)} %get-tuple-element.280) | copy-start | bytes 3145732
Sparse Core Ops, SparseCore 0:
  316.7 40.9 all-reduce.6
  364.4 236.4 all-reduce.4
